TPU v7x, 32 devices: a whole 2x2x4 slice. The times are simulated.
32 devices in a mesh: groups: 2 (over y), wide: 4 (over z), narrow: 2 (over x), sub: 2 (over core).
Axes of the slice: x: 2, y: 2, z: 4, core: 2. Of those that a mesh axis runs over, the one named last changes fastest.
Arguments:
- tokens: bfloat16 [128, 8192], P(('groups', 'wide', 'sub'), 'narrow'), parts along dimension 0, may hold values from -6 to 6
- gate_weight: bfloat16 [8192, 26624], P('narrow', ('wide', 'sub')), may hold values from -0.0625 to 0.0625
- up_weight: bfloat16 [8192, 26624], P('narrow', ('wide', 'sub')), may hold values from -0.0625 to 0.0625
- down_weight: bfloat16 [26624, 8192], P(('wide', 'sub'), 'narrow'), may hold values from -0.0390625 to 0.0390625
Outputs:
- block_out: bfloat16 [128, 8192], P(('groups', 'wide', 'sub'), 'narrow'), parts along dimension 0
There are 2 independent parts, one for each index of `groups`. A program takes and returns all parts, laid end to end along the dimension named above; an argument that names none is the same for every part. Nothing has to cross between parts.
All inputs are finite; a program needn't handle non-finite values.
Results may differ from a plain program's by a relative error of at most 0.005.
Values may be sent and summed in bfloat16 or wider, within the bound.
A program may use at most 192 MiB of HBM per device.

v0:
```python
import jax
import jax.numpy as jnp
from jax import lax
from jax.sharding import PartitionSpec as P


def per_device(tokens, gate_weight, up_weight, down_weight):
    segment = lax.all_gather(tokens, ("wide", "sub"), axis=0, tiled=True)
    gate_part = jnp.dot(segment, gate_weight, preferred_element_type=jnp.float32)
    up_part = jnp.dot(segment, up_weight, preferred_element_type=jnp.float32)
    partial_value = jnp.stack([gate_part, up_part])
    totals = lax.psum(partial_value, "narrow")
    hidden = (jax.nn.silu(totals[0]) * totals[1]).astype(jnp.bfloat16)
    output_block = lax.psum_scatter(
        jnp.dot(hidden, down_weight, preferred_element_type=jnp.float32),
        ("wide", "sub"),
        scatter_dimension=0,
        tiled=True,
    )
    return output_block.astype(jnp.bfloat16)


def solution(mesh):
    return jax.shard_map(
        per_device,
        mesh=mesh,
        in_specs=(
            P(("groups", "wide", "sub"), "narrow"),
            P("narrow", ("wide", "sub")),
            P("narrow", ("wide", "sub")),
            P(("wide", "sub"), "narrow"),
        ),
        out_specs=P(("groups", "wide", "sub"), "narrow"),
        check_vma=False,
    )
```

profile of v0, /device:TPU:0, one launch (start us, length us, event | category | flops | bytes accessed | tf_op | source)
XLA Modules:
  0.0 158.7 jit_solution(8538847101970778802)
XLA Ops:
  6.5 0.0 all-reduce.2.cloned.1.call-start
  6.5 16.8 %all_gather.3 = bf16[64,4096]{1,0:T(8,128)(2,1)S(1)} all-gather(bf16[8,4096]{1,0:T(8,128)(2,1)} %param.4), channel_id=1, replica_groups=mesh['groups'=2,'wide'=4,'narrow'=2,'sub'=2] {'wide','sub'}, dimensions={0}, use_global_device_ids=true | all-gather | bytes 589824 | tf_op jit(solution)/shard_map/all_gather | solution.py:8
  23.3 11.2 %convolution_bitcast_fusion = f32[1,64,3328]{2,1,0:T(8,128)S(1)} fusion(bf16[64,4096]{1,0:T(8,128)(2,1)S(1)} %all_gather.3, bf16[4096,3328]{1,0:T(8,128)(2,1)} %param.6), kind=kOutput, calls=%fused_computation | convolution fusion | flops 1744830464 | bytes 28639232 | tf_op jit(solution)/shard_map/dot_general | solution.py:10
  34.5 11.2 %convolution_bitcast_fusion.1 = f32[1,64,3328]{2,1,0:T(8,128)S(1)} fusion(bf16[64,4096]{1,0:T(8,128)(2,1)S(1)} %all_gather.3, bf16[4096,3328]{1,0:T(8,128)(2,1)} %param.5), kind=kOutput, calls=%fused_computation.1 | convolution fusion | flops 1744830464 | bytes 28639232 | tf_op jit(solution)/shard_map/dot_general | solution.py:9
  45.7 1.3 pad_maximum_fusion
  47.0 0.0 all-reduce.2.cloned.1.call-update
  47.1 0.0 reduce-scatter.2.cloned.1.call-start
  47.1 55.5 %all-reduce.2.cloned.1.call-done = f32[2,64,3328]{2,1,0:T(8,128)} async-done(((f32[2,64,3328]{2,1,0:T(8,128)}), f32[2,64,3328]{2,1,0:T(8,128)}) %all-reduce.2.cloned.1.call-update) | async-done | bytes 1703952 | tf_op jit(solution)/shard_map/psum | solution.py:12
  102.6 15.1 %fusion.2 = f32[64,4096]{1,0:T(8,128)} fusion(bf16[3328,4096]{1,0:T(8,128)(2,1)} %param.7, f32[2,64,3328]{2,1,0:T(8,128)} %all-reduce.2.cloned.1.call-done), kind=kOutput, calls=%fused_computation.7 | convolution fusion | flops 1746108416 | bytes 30015488 | tf_op jit(solution)/shard_map/dot_general | solution.py:15
  117.7 0.0 reduce-scatter.2.cloned.1.call-update
  117.7 32.6 %reduce-scatter.2.cloned.1.call-done = f32[8,4096]{1,0:T(8,128)} async-done(((f32[64,4096]{1,0:T(8,128)}), f32[8,4096]{1,0:T(8,128)}) %reduce-scatter.2.cloned.1.call-update) | async-done | bytes 131088 | tf_op jit(solution)/shard_map/reduce_scatter | solution.py:14
  150.3 1.5 convert_element_type.7
Async XLA Ops:
  6.5 96.1 %all-reduce.2.cloned.1.call-start = ((), (), s32[]{:S(2)}) async-start(), calls=%async_computation.1 | async-start | bytes 3407872 | tf_op jit(solution)/shard_map/psum | solution.py:12
  47.1 103.2 %reduce-scatter.2.cloned.1.call-start = ((), (), s32[]{:S(2)}) async-start(), calls=%async_computation.2 | async-start | bytes 1179648 | tf_op jit(solution)/shard_map/reduce_scatter | solution.py:14
Sparse Core Ops, SparseCore 0:
  47.2 55.3 all-reduce.1
  117.8 32.4 reduce-scatter.1
where the time goes:
time: 159 us
  waiting for transfers between devices  88.1 us (55%)
  matrix products  37.5 us (24%)
  blocking collectives  16.8 us (11%)
  between operations  13.4 us (8%)
  other arithmetic  2.84 us (2%)
    psum x1, waiting for transfers between devices, per_device(): totals = lax.psum(partial_value, 'narrow')  55.5 us
    reduce_scatter x1, waiting for transfers between devices, per_device(): lax.psum_scatter(jnp.dot(hidden, down_weight, preferred_element_type=jnp....  32.6 us
    all_gather x1, blocking collectives, per_device(): segment = lax.all_gather(tokens, ('wide', 'sub'), axis=0, tiled=True)  16.8 us
    dot_general x1, matrix products, per_device(): jnp.dot(hidden, down_weight, preferred_element_type=jnp.float32)  15.1 us
    dot_general x1, matrix products, per_device(): jnp.dot(segment, gate_weight, preferred_element_type=jnp.float32)  11.2 us
    dot_general x1, matrix products, per_device(): up_part = jnp.dot(segment, up_weight, preferred_element_type=jnp.float32)  11.2 us
  transfers between devices with their start and end apart: 2, of which 2 were waited for; matrix products, arithmetic and copies ran while one was open for 0% of the time, Pallas kernels for 0%

commit v1 on v0

v1 whole, which is shorter than its diff:
```python
import functools

import jax
import jax.numpy as jnp
from jax import lax
from jax.experimental import pallas as pl
from jax.experimental.pallas import tpu as pltpu
from jax.sharding import PartitionSpec as P

MESH = pl.DeviceIdType.MESH
F32 = jnp.float32
BF16 = jnp.bfloat16


def plain(tokens, gate_weight, up_weight, down_weight):
    segment = lax.all_gather(tokens, ("wide", "sub"), axis=0, tiled=True)
    gate_part = jnp.dot(segment, gate_weight, preferred_element_type=F32)
    up_part = jnp.dot(segment, up_weight, preferred_element_type=F32)
    totals = lax.psum(jnp.stack([gate_part, up_part]), "narrow")
    hidden = (jax.nn.silu(totals[0]) * totals[1]).astype(BF16)
    output_block = lax.psum_scatter(
        jnp.dot(hidden, down_weight, preferred_element_type=F32),
        ("wide", "sub"),
        scatter_dimension=0,
        tiled=True,
    )
    return output_block.astype(BF16)


def chunks_of(extent, width):
    return [(o, min(width, extent - o)) for o in range(0, extent, width)]


def kernel(W, chunks, down_groups, tiles,
           x_ref, gate_ref, up_ref, down_ref, out_ref,
           wg, wu, wd, tok, T, own, xsend, xrecv, hid, acc, srecv, ysend, yrecv, oacc, zsend, zrecv,
           wg_sem, wu_sem, wd_sem, tz_s, ty_s, tc_s, t_r, p_s, p_r, h_s, h_r,
           s_s, s_r, y_s, y_r, z_s, z_r):
    g, w, n, s = (lax.axis_index(a) for a in ("groups", "wide", "narrow", "sub"))
    B, D = x_ref.shape
    HU = wg.shape[1]
    R = T.shape[0]
    R2, R4 = R // 2, R // 4

    def weight_copy(src, dst, sems, c, rows):
        o, k = chunks[c]
        at = pl.ds(pl.multiple_of(g * HU + o, 128), k)
        if rows:
            return pltpu.make_async_copy(src.at[at, :], dst.at[pl.ds(o, k), :], sems.at[c])
        return pltpu.make_async_copy(src.at[:, at], dst.at[:, pl.ds(o, k)], sems.at[c])

    gates = [weight_copy(gate_ref, wg, wg_sem, c, False) for c in range(len(chunks))]
    ups = [weight_copy(up_ref, wu, wu_sem, c, False) for c in range(len(chunks))]
    downs = [weight_copy(down_ref, wd, wd_sem, c, True) for c in range(len(chunks))]
    for c in range(len(chunks)):
        gates[c].start()
        ups[c].start()
    for d in downs:
        d.start()

    def remote(src, dst, send, recv, **to):
        return pltpu.make_async_remote_copy(
            src_ref=src, dst_ref=dst, send_sem=send, recv_sem=recv, device_id=to, device_id_type=MESH)

    others = [lax.rem(w + d, W) for d in range(1, W)]
    barrier = pltpu.get_barrier_semaphore()
    for to in [{"wide": o} for o in others] + [{"groups": 1 - g}, {"sub": 1 - s}, {"narrow": 1 - n}]:
        pl.semaphore_signal(barrier, inc=1, device_id=to, device_id_type=MESH)
    x = x_ref[...].astype(F32)
    block = lambda gg, ww, ss: ss * (2 * W) + gg * W + ww
    me = block(g, w, s)
    tok[me] = jnp.concatenate([x[:, : D // 2], x[:, D // 2:]], axis=0).astype(BF16)
    pl.semaphore_wait(barrier, W + 2)

    sends = []

    def go(copy):
        copy.start()
        sends.append(copy)

    def to_z(b, o):
        return remote(tok.at[b], tok.at[b], tz_s.at[o], t_r.at[b], wide=o)

    def to_y(b, o):
        return remote(tok.at[b], tok.at[b], ty_s.at[o], t_r.at[b], groups=1 - g)

    def to_core(b, i):
        return remote(tok.at[b], tok.at[b], tc_s.at[i], t_r.at[b], sub=1 - s)

    for o in others:
        go(to_z(me, o))
    go(to_y(me, w))
    go(to_core(me, g * W + w))
    for o in others:
        b = block(g, o, s)
        to_z(b, o).wait_recv()
        go(to_y(b, o))
        go(to_core(b, g * W + o))
    for o in [w] + others:
        b = block(1 - g, o, s)
        to_y(b, o).wait_recv()
        go(to_core(b, (1 - g) * W + o))
    for gg in range(2):
        for ww in range(W):
            to_core(block(gg, ww, 1 - s), gg * W + ww).wait_recv()

    for j in range(R // 16):
        a = tok[2 * j].astype(F32)
        b = tok[2 * j + 1].astype(F32)
        T[16 * j:16 * j + 16, : D // 2] = jnp.concatenate([a[:B], b[:B]], axis=0).astype(BF16)
        T[16 * j:16 * j + 16, D // 2:] = jnp.concatenate([a[B:], b[B:]], axis=0).astype(BF16)

    mine = pl.ds(pl.multiple_of(n * R2, R2), R2)

    def partial(c):
        at = pl.ds(chunks[c][0], chunks[c][1])
        return remote(xsend.at[:, :, at], xrecv.at[:, :, at], p_s.at[c], p_r.at[c], narrow=1 - n)

    def spread(c):
        at = pl.ds(chunks[c][0], chunks[c][1])
        return remote(hid.at[mine, at], hid.at[mine, at], h_s.at[c], h_r.at[c], narrow=1 - n)

    def widen(c):
        o, k = chunks[c]
        at = slice(o, o + k)
        for i, (wait, ref) in enumerate(((gates[c], wg), (ups[c], wu))):
            wait.wait()
            r = jnp.dot(T[...], ref[:, at], preferred_element_type=F32)
            first = n == 0
            own[i, :, at] = jnp.where(first, r[:R2], r[R2:])
            xsend[i, :, at] = jnp.where(first, r[R2:], r[:R2]).astype(BF16)
        go(partial(c))

    def activate(c):
        o, k = chunks[c]
        at = slice(o, o + k)
        partial(c).wait_recv()
        a = own[0, :, at] + xrecv[0, :, at].astype(F32)
        b = own[1, :, at] + xrecv[1, :, at].astype(F32)
        hid[mine, at] = (a / (1.0 + jnp.exp(-a)) * b).astype(BF16)
        go(spread(c))

    def narrow_down(i, after=None):
        group = down_groups[i]
        for c in group:
            downs[c].wait()
            spread(c).wait_recv()
        lo, hi = chunks[group[0]][0], chunks[group[-1]][0] + chunks[group[-1]][1]
        for t, (o, k) in enumerate(tiles):
            r = jnp.dot(hid[:, lo:hi], wd[lo:hi, o:o + k], preferred_element_type=F32)
            if i > 0:
                r = r + acc[:, o:o + k]
            acc[:, o:o + k] = r
            if after is not None:
                after(t)

    lag = 2
    C = len(chunks)
    ready = {grp[-1]: i for i, grp in enumerate(down_groups)}
    last = len(down_groups) - 1

    def core_sum(t):
        at = pl.ds(*tiles[t])
        theirs = pl.ds(pl.multiple_of((1 - s) * R2, R2), R2)
        return remote(acc.at[theirs, at], srecv.at[:, at], s_s.at[t], s_r.at[t], sub=1 - s)

    def y_sum(t):
        at = pl.ds(*tiles[t])
        return remote(ysend.at[:, at], yrecv.at[:, at], y_s.at[t], y_r.at[t], groups=1 - g)

    for c in range(C + lag + 2):
        if c < C:
            widen(c)
        if 0 <= c - lag < C:
            activate(c - lag)
        i = ready.get(c - lag - 2)
        if i is not None:
            narrow_down(i, (lambda t: go(core_sum(t))) if i == last else None)

    def rows(base):
        return pl.ds(pl.multiple_of(base, R4), R4)

    for t, (o, k) in enumerate(tiles):
        core_sum(t).wait_recv()
        at = slice(o, o + k)
        ysend[:, at] = (acc[rows(s * R2 + (1 - g) * R4), at] + srecv[rows((1 - g) * R4), at]).astype(BF16)
        go(y_sum(t))

    def z_send(t, o):
        return remote(zsend.at[t, o], zrecv.at[t, w], z_s.at[t, o], z_r.at[t, w], wide=o)

    def z_arrival(t, o):
        return remote(zsend.at[t, o], zrecv.at[t, o], z_s.at[t, o], z_r.at[t, o], wide=o)

    for t, (o, k) in enumerate(tiles):
        y_sum(t).wait_recv()
        at = slice(o, o + k)
        r = acc[rows(s * R2 + g * R4), at] + srecv[rows(g * R4), at] + yrecv[:, at].astype(F32)
        oacc[:, at] = r
        for ww in range(W):
            v = r[ww * B:(ww + 1) * B]
            zsend[t, ww] = jnp.concatenate([v[:, : k // 2], v[:, k // 2:]], axis=0).astype(BF16)
        for p in others:
            go(z_send(t, p))

    for t, (o, k) in enumerate(tiles):
        r = oacc[pl.ds(pl.multiple_of(w * B, B), B), o:o + k]
        for p in others:
            z_arrival(t, p).wait_recv()
            v = zrecv[t, p].astype(F32)
            r = r + jnp.concatenate([v[:B], v[B:]], axis=1)
        out_ref[:, o:o + k] = r.astype(BF16)

    for copy in sends:
        copy.wait_send()


def fused(W, tokens, gate_weight, up_weight, down_weight):
    B, D = tokens.shape
    H = gate_weight.shape[1]
    HU = H // 2
    N = down_weight.shape[1]
    R = 4 * W * B
    chunks = chunks_of(HU, 256)
    C = len(chunks)
    down_groups = [tuple(range(i, min(i + 2, C))) for i in range(0, C, 2)]
    tiles = chunks_of(N, 1024)
    NT = len(tiles)
    dma = pltpu.SemaphoreType.DMA
    scratch = [
        pltpu.VMEM((D, HU), BF16), pltpu.VMEM((D, HU), BF16), pltpu.VMEM((HU, N), BF16),
        pltpu.VMEM((4 * W, 2 * B, D // 2), BF16), pltpu.VMEM((R, D), BF16),
        pltpu.VMEM((2, R // 2, HU), F32), pltpu.VMEM((2, R // 2, HU), BF16), pltpu.VMEM((2, R // 2, HU), BF16),
        pltpu.VMEM((R, HU), BF16), pltpu.VMEM((R, N), F32), pltpu.VMEM((R // 2, N), F32),
        pltpu.VMEM((R // 4, N), BF16), pltpu.VMEM((R // 4, N), BF16), pltpu.VMEM((R // 4, N), F32),
        pltpu.VMEM((NT, W, 2 * B, tiles[0][1] // 2), BF16), pltpu.VMEM((NT, W, 2 * B, tiles[0][1] // 2), BF16),
        dma((C,)), dma((C,)), dma((C,)),
        dma((W,)), dma((W,)), dma((2 * W,)), dma((4 * W,)),
        dma((C,)), dma((C,)), dma((C,)), dma((C,)),
        dma((NT,)), dma((NT,)), dma((NT,)), dma((NT,)), dma((NT, W)), dma((NT, W)),
    ]
    vmem, hbm = pl.BlockSpec(memory_space=pltpu.VMEM), pl.BlockSpec(memory_space=pl.ANY)
    return pl.pallas_call(
        functools.partial(kernel, W, chunks, down_groups, tiles),
        out_shape=jax.ShapeDtypeStruct((B, N), BF16),
        in_specs=[vmem, hbm, hbm, hbm],
        out_specs=vmem,
        scratch_shapes=scratch,
        compiler_params=pltpu.CompilerParams(
            collective_id=0, has_side_effects=True, vmem_limit_bytes=60 * 2**20),
        cost_estimate=pl.CostEstimate(
            flops=6 * R * D * HU, bytes_accessed=6 * D * HU, transcendentals=R * HU // 2),
    )(tokens, gate_weight, up_weight, down_weight)


def fits(mesh, tokens, gate_weight, down_weight):
    size = mesh.shape
    rows, hidden, columns = tokens.shape[0], gate_weight.shape[1], down_weight.shape[1]
    return (
        size["groups"] == 2 and size["narrow"] == 2 and size["sub"] == 2 and size["wide"] <= 4
        and rows == 8 and hidden % 256 == 0 and columns % 1024 == 0
        and 3 * tokens.shape[1] * hidden <= 48 * 2**20
    )


def solution(mesh):
    def per_device(tokens, gate_weight, up_weight, down_weight):
        if fits(mesh, tokens, gate_weight, down_weight):
            return fused(mesh.shape["wide"], tokens, gate_weight, up_weight, down_weight)
        return plain(tokens, gate_weight, up_weight, down_weight)

    return jax.shard_map(
        per_device,
        mesh=mesh,
        in_specs=(
            P(("groups", "wide", "sub"), "narrow"),
            P("narrow", ("wide", "sub")),
            P("narrow", ("wide", "sub")),
            P(("wide", "sub"), "narrow"),
        ),
        out_specs=P(("groups", "wide", "sub"), "narrow"),
        check_vma=False,
    )
```

time: 159 us -> 52.4 us (0.33)
  waiting for transfers between devices: 88.1 us -> 0 us
  Pallas kernels: 0 us -> 50.7 us
  matrix products: 37.5 us -> 0 us
  blocking collectives: 16.8 us -> 0 us
  between operations: 13.4 us -> 0.01 us
  other arithmetic: 2.84 us -> 0 us
    psum x1 -> x0, waiting for transfers between devices: 55.5 us -> none  [per_device(): totals = lax.psum(partial_value, 'narrow')]
    pallas_call x0 -> x1, Pallas kernels: none -> 50.7 us  [fused(): pl.pallas_call(functools.partial(kernel, W, chunks, down_groups, tiles),...]
    dot_general x3 -> x0, matrix products: 37.5 us -> none  [the longest x1 15.1 us: per_device(): jnp.dot(hidden, down_weight, preferred_element_type=jnp.float32)]
    reduce_scatter x1 -> x0, waiting for transfers between devices: 32.6 us -> none  [per_device(): lax.psum_scatter(jnp.dot(hidden, down_weight, preferred_element_type=jnp....]
    all_gather x1 -> x0, blocking collectives: 16.8 us -> none  [per_device(): segment = lax.all_gather(tokens, ('wide', 'sub'), axis=0, tiled=True)]
  transfers between devices with their start and end apart: 2 -> 0, of which waited for: 2 -> 0; matrix products, arithmetic and copies ran while one was open for 0% -> 0% of each run, Pallas kernels for 0% -> 0%
where the time goes in v1:
time: 52.4 us; the launch traced here: 52.2 us
  Pallas kernels  50.7 us (97%)
  local copies, waits for them, and re-layouts  1.47 us (3%)
    pallas_call x1, Pallas kernels, fused(): pl.pallas_call(functools.partial(kernel, W, chunks, down_groups, tiles),...  50.7 us
    unnamed x1, local copies, waits for them, and re-layouts  1.47 us

profile of v1, /device:TPU:0, one launch (start us, length us, event | category | flops | bytes accessed | tf_op | source)
XLA Modules:
  0.0 52.2 jit_solution(4970031261410794701)
XLA Ops:
  0.0 50.7 %shard_map.46 = bf16[8,4096]{1,0:T(8,128)(2,1)} custom-call(bf16[8,4096]{1,0:T(8,128)(2,1)} %x_ref.1, bf16[4096,3328]{1,0:T(8,128)(2,1)} %gate_ref.1, bf16[4096,3328]{1,0:T(8,128)(2,1)} %up_ref.1, bf16[3328,4096]{1,0:T(8,128)(2,1)} %down_ref.1), custom_call_target="tpu_custom_call" | custom-call | flops 5234491392 | bytes 40894464 | tf_op jit(solution)/shard_map/pallas_call | solution.py:243
  50.7 1.5 %copy.6 = bf16[8,4096]{1,0:T(8,128)(2,1)} copy(bf16[8,4096]{1,0:T(8,128)(2,1)} %shard_map.46) | data formatting | bytes 131072

commit v2 on v1

--- a/solution.py
+++ b/solution.py
@@ -110,98 +110,118 @@
         T[16 * j:16 * j + 16, : D // 2] = jnp.concatenate([a[:B], b[:B]], axis=0).astype(BF16)
         T[16 * j:16 * j + 16, D // 2:] = jnp.concatenate([a[B:], b[B:]], axis=0).astype(BF16)
 
-    mine = pl.ds(pl.multiple_of(n * R2, R2), R2)
-
-    def partial(c):
+    def mine(h):
+        return pl.ds(pl.multiple_of(h * R2 + n * R4, R4), R4)
+
+    C = len(chunks)
+
+    def partial(h, c):
         at = pl.ds(chunks[c][0], chunks[c][1])
-        return remote(xsend.at[:, :, at], xrecv.at[:, :, at], p_s.at[c], p_r.at[c], narrow=1 - n)
-
-    def spread(c):
+        return remote(xsend.at[h, :, :, at], xrecv.at[h, :, :, at], p_s.at[h, c], p_r.at[h, c], narrow=1 - n)
+
+    def spread(h, c):
         at = pl.ds(chunks[c][0], chunks[c][1])
-        return remote(hid.at[mine, at], hid.at[mine, at], h_s.at[c], h_r.at[c], narrow=1 - n)
-
-    def widen(c):
+        return remote(hid.at[mine(h), at], hid.at[mine(h), at], h_s.at[h, c], h_r.at[h, c], narrow=1 - n)
+
+    def widen(h, c):
         o, k = chunks[c]
         at = slice(o, o + k)
-        for i, (wait, ref) in enumerate(((gates[c], wg), (ups[c], wu))):
-            wait.wait()
-            r = jnp.dot(T[...], ref[:, at], preferred_element_type=F32)
-            first = n == 0
-            own[i, :, at] = jnp.where(first, r[:R2], r[R2:])
-            xsend[i, :, at] = jnp.where(first, r[R2:], r[:R2]).astype(BF16)
-        go(partial(c))
-
-    def activate(c):
+        if h == 0:
+            gates[c].wait()
+            ups[c].wait()
+        first = n == 0
+        for i, ref in enumerate((wg, wu)):
+            r = jnp.dot(T[h * R2:(h + 1) * R2, :], ref[:, at], preferred_element_type=F32)
+            own[h, i, :, at] = jnp.where(first, r[:R4], r[R4:])
+            xsend[h, i, :, at] = jnp.where(first, r[R4:], r[:R4]).astype(BF16)
+        go(partial(h, c))
+
+    def activate(h, c):
         o, k = chunks[c]
         at = slice(o, o + k)
-        partial(c).wait_recv()
-        a = own[0, :, at] + xrecv[0, :, at].astype(F32)
-        b = own[1, :, at] + xrecv[1, :, at].astype(F32)
-        hid[mine, at] = (a / (1.0 + jnp.exp(-a)) * b).astype(BF16)
-        go(spread(c))
-
-    def narrow_down(i, after=None):
-        group = down_groups[i]
-        for c in group:
-            downs[c].wait()
-            spread(c).wait_recv()
-        lo, hi = chunks[group[0]][0], chunks[group[-1]][0] + chunks[group[-1]][1]
-        for t, (o, k) in enumerate(tiles):
-            r = jnp.dot(hid[:, lo:hi], wd[lo:hi, o:o + k], preferred_element_type=F32)
-            if i > 0:
-                r = r + acc[:, o:o + k]
-            acc[:, o:o + k] = r
-            if after is not None:
-                after(t)
-
-    lag = 2
-    C = len(chunks)
-    ready = {grp[-1]: i for i, grp in enumerate(down_groups)}
-    last = len(down_groups) - 1
+        partial(h, c).wait_recv()
+        a = own[h, 0, :, at] + xrecv[h, 0, :, at].astype(F32)
+        b = own[h, 1, :, at] + xrecv[h, 1, :, at].astype(F32)
+        hid[mine(h), at] = (a / (1.0 + jnp.exp(-a)) * b).astype(BF16)
+        go(spread(h, c))
 
     def core_sum(t):
         at = pl.ds(*tiles[t])
         theirs = pl.ds(pl.multiple_of((1 - s) * R2, R2), R2)
         return remote(acc.at[theirs, at], srecv.at[:, at], s_s.at[t], s_r.at[t], sub=1 - s)
 
+    def narrow_down(h, i):
+        group = down_groups[i]
+        for c in group:
+            if h == 0:
+                downs[c].wait()
+            spread(h, c).wait_recv()
+        lo, hi = chunks[group[0]][0], chunks[group[-1]][0] + chunks[group[-1]][1]
+        half = slice(h * R2, (h + 1) * R2)
+        for t, (base, k) in enumerate(tiles):
+            for o in range(base, base + k, 1024):
+                r = jnp.dot(hid[half, lo:hi], wd[lo:hi, o:o + 1024], preferred_element_type=F32)
+                if i > 0:
+                    r = r + acc[half, o:o + 1024]
+                acc[half, o:o + 1024] = r
+            if i == len(down_groups) - 1:
+                @pl.when(s != h)
+                def _():
+                    core_sum(t).start()
+
+    def rows(base):
+        return pl.ds(pl.multiple_of(base, R4), R4)
+
     def y_sum(t):
         at = pl.ds(*tiles[t])
         return remote(ysend.at[:, at], yrecv.at[:, at], y_s.at[t], y_r.at[t], groups=1 - g)
 
-    for c in range(C + lag + 2):
-        if c < C:
-            widen(c)
-        if 0 <= c - lag < C:
-            activate(c - lag)
-        i = ready.get(c - lag - 2)
-        if i is not None:
-            narrow_down(i, (lambda t: go(core_sum(t))) if i == last else None)
-
-    def rows(base):
-        return pl.ds(pl.multiple_of(base, R4), R4)
-
-    for t, (o, k) in enumerate(tiles):
-        core_sum(t).wait_recv()
-        at = slice(o, o + k)
-        ysend[:, at] = (acc[rows(s * R2 + (1 - g) * R4), at] + srecv[rows((1 - g) * R4), at]).astype(BF16)
-        go(y_sum(t))
-
     def z_send(t, o):
         return remote(zsend.at[t, o], zrecv.at[t, w], z_s.at[t, o], z_r.at[t, w], wide=o)
 
     def z_arrival(t, o):
         return remote(zsend.at[t, o], zrecv.at[t, o], z_s.at[t, o], z_r.at[t, o], wide=o)
 
-    for t, (o, k) in enumerate(tiles):
-        y_sum(t).wait_recv()
-        at = slice(o, o + k)
-        r = acc[rows(s * R2 + g * R4), at] + srecv[rows(g * R4), at] + yrecv[:, at].astype(F32)
-        oacc[:, at] = r
-        for ww in range(W):
-            v = r[ww * B:(ww + 1) * B]
-            zsend[t, ww] = jnp.concatenate([v[:, : k // 2], v[:, k // 2:]], axis=0).astype(BF16)
-        for p in others:
-            go(z_send(t, p))
+    def over_y(h):
+        for t, (o, k) in enumerate(tiles):
+            core_sum(t).wait_recv()
+            at = slice(o, o + k)
+            ysend[:, at] = (acc[rows(h * R2 + (1 - g) * R4), at] + srecv[rows((1 - g) * R4), at]).astype(BF16)
+            y_sum(t).start()
+
+    def over_z(h):
+        for t, (o, k) in enumerate(tiles):
+            y_sum(t).wait_recv()
+            at = slice(o, o + k)
+            r = acc[rows(h * R2 + g * R4), at] + srecv[rows(g * R4), at] + yrecv[:, at].astype(F32)
+            oacc[:, at] = r
+            for ww in range(W):
+                v = r[ww * B:(ww + 1) * B]
+                zsend[t, ww] = jnp.concatenate([v[:, : k // 2], v[:, k // 2:]], axis=0).astype(BF16)
+            for d in range(1, W):
+                z_send(t, lax.rem(w + d, W)).start()
+
+    steps = [(h, c) for h in range(2) for c in range(C)]
+    ready = {grp[-1]: i for i, grp in enumerate(down_groups)}
+    lag = 2
+    for q in range(len(steps) + 2 * lag):
+        if q < len(steps):
+            widen(*steps[q])
+        if 0 <= q - lag < len(steps):
+            activate(*steps[q - lag])
+        if 0 <= q - 2 * lag < len(steps):
+            h, c = steps[q - 2 * lag]
+            if c in ready:
+                narrow_down(h, ready[c])
+            if (h, c) == (1, 0):
+                pl.when(s == 0)(lambda: over_y(0))
+            if (h, c) == (1, C - 2):
+                pl.when(s == 0)(lambda: over_z(0))
+
+    @pl.when(s == 1)
+    def _():
+        over_y(1)
+        over_z(1)
 
     for t, (o, k) in enumerate(tiles):
         r = oacc[pl.ds(pl.multiple_of(w * B, B), B), o:o + k]
@@ -213,6 +233,11 @@
 
     for copy in sends:
         copy.wait_send()
+    for t in range(len(tiles)):
+        core_sum(t).wait_send()
+        y_sum(t).wait_send()
+        for p in others:
+            z_send(t, p).wait_send()
 
 
 def fused(W, tokens, gate_weight, up_weight, down_weight):
@@ -221,22 +246,22 @@
     HU = H // 2
     N = down_weight.shape[1]
     R = 4 * W * B
-    chunks = chunks_of(HU, 256)
+    chunks = chunks_of(HU, 512)
     C = len(chunks)
-    down_groups = [tuple(range(i, min(i + 2, C))) for i in range(0, C, 2)]
-    tiles = chunks_of(N, 1024)
+    down_groups = [(0, 1)] + [(c,) for c in range(2, C)]
+    tiles = chunks_of(N, 2048)
     NT = len(tiles)
     dma = pltpu.SemaphoreType.DMA
     scratch = [
         pltpu.VMEM((D, HU), BF16), pltpu.VMEM((D, HU), BF16), pltpu.VMEM((HU, N), BF16),
         pltpu.VMEM((4 * W, 2 * B, D // 2), BF16), pltpu.VMEM((R, D), BF16),
-        pltpu.VMEM((2, R // 2, HU), F32), pltpu.VMEM((2, R // 2, HU), BF16), pltpu.VMEM((2, R // 2, HU), BF16),
+        pltpu.VMEM((2, 2, R // 4, HU), F32), pltpu.VMEM((2, 2, R // 4, HU), BF16), pltpu.VMEM((2, 2, R // 4, HU), BF16),
         pltpu.VMEM((R, HU), BF16), pltpu.VMEM((R, N), F32), pltpu.VMEM((R // 2, N), F32),
         pltpu.VMEM((R // 4, N), BF16), pltpu.VMEM((R // 4, N), BF16), pltpu.VMEM((R // 4, N), F32),
         pltpu.VMEM((NT, W, 2 * B, tiles[0][1] // 2), BF16), pltpu.VMEM((NT, W, 2 * B, tiles[0][1] // 2), BF16),
         dma((C,)), dma((C,)), dma((C,)),
         dma((W,)), dma((W,)), dma((2 * W,)), dma((4 * W,)),
-        dma((C,)), dma((C,)), dma((C,)), dma((C,)),
+        dma((2, C)), dma((2, C)), dma((2, C)), dma((2, C)),
         dma((NT,)), dma((NT,)), dma((NT,)), dma((NT,)), dma((NT, W)), dma((NT, W)),
     ]
     vmem, hbm = pl.BlockSpec(memory_space=pltpu.VMEM), pl.BlockSpec(memory_space=pl.ANY)
@@ -258,7 +283,7 @@
     rows, hidden, columns = tokens.shape[0], gate_weight.shape[1], down_weight.shape[1]
     return (
         size["groups"] == 2 and size["narrow"] == 2 and size["sub"] == 2 and size["wide"] <= 4
-        and rows == 8 and hidden % 256 == 0 and columns % 1024 == 0
+        and rows == 8 and size["wide"] % 4 == 0 and hidden % 256 == 0 and hidden >= 2048 and columns % 2048 == 0
         and 3 * tokens.shape[1] * hidden <= 48 * 2**20
     )
 

time: 52.4 us -> 53 us (1.011)
  the two profiles are of different devices: /device:TPU:0 before, /device:TPU:1 now
where the time goes in v2:
time: 53 us; the launch traced here: 52.8 us
  Pallas kernels  51.3 us (97%)
  local copies, waits for them, and re-layouts  1.47 us (3%)
    pallas_call x1, Pallas kernels, fused(): pl.pallas_call(functools.partial(kernel, W, chunks, down_groups, tiles),...  51.3 us
    unnamed x1, local copies, waits for them, and re-layouts  1.47 us

profile of v2, /device:TPU:1, one launch (start us, length us, event | category | flops | bytes accessed | tf_op | source)
XLA Modules:
  0.0 52.8 jit_solution(7770053306662831778)
XLA Ops:
  0.0 51.3 %shard_map.46 = bf16[8,4096]{1,0:T(8,128)(2,1)} custom-call(bf16[8,4096]{1,0:T(8,128)(2,1)} %x_ref.1, bf16[4096,3328]{1,0:T(8,128)(2,1)} %gate_ref.1, bf16[4096,3328]{1,0:T(8,128)(2,1)} %up_ref.1, bf16[3328,4096]{1,0:T(8,128)(2,1)} %down_ref.1), custom_call_target="tpu_custom_call" | custom-call | flops 5234491392 | bytes 40894464 | tf_op jit(solution)/shard_map/pallas_call | solution.py:268
  51.3 1.5 %copy.6 = bf16[8,4096]{1,0:T(8,128)(2,1)} copy(bf16[8,4096]{1,0:T(8,128)(2,1)} %shard_map.46) | data formatting | bytes 131072

commit v3 on v1

--- a/solution.py
+++ b/solution.py
@@ -42,6 +42,11 @@
     R = T.shape[0]
     R2, R4 = R // 2, R // 4
 
+    others = [lax.rem(w + d, W) for d in range(1, W)]
+    barrier = pltpu.get_barrier_semaphore()
+    for to in [{"wide": o} for o in others] + [{"groups": 1 - g}, {"sub": 1 - s}, {"narrow": 1 - n}]:
+        pl.semaphore_signal(barrier, inc=1, device_id=to, device_id_type=MESH)
+
     def weight_copy(src, dst, sems, c, rows):
         o, k = chunks[c]
         at = pl.ds(pl.multiple_of(g * HU + o, 128), k)
@@ -62,10 +67,6 @@
         return pltpu.make_async_remote_copy(
             src_ref=src, dst_ref=dst, send_sem=send, recv_sem=recv, device_id=to, device_id_type=MESH)
 
-    others = [lax.rem(w + d, W) for d in range(1, W)]
-    barrier = pltpu.get_barrier_semaphore()
-    for to in [{"wide": o} for o in others] + [{"groups": 1 - g}, {"sub": 1 - s}, {"narrow": 1 - n}]:
-        pl.semaphore_signal(barrier, inc=1, device_id=to, device_id_type=MESH)
     x = x_ref[...].astype(F32)
     block = lambda gg, ww, ss: ss * (2 * W) + gg * W + ww
     me = block(g, w, s)
@@ -123,8 +124,9 @@
     def widen(c):
         o, k = chunks[c]
         at = slice(o, o + k)
-        for i, (wait, ref) in enumerate(((gates[c], wg), (ups[c], wu))):
-            wait.wait()
+        gates[c].wait()
+        ups[c].wait()
+        for i, ref in enumerate((wg, wu)):
             r = jnp.dot(T[...], ref[:, at], preferred_element_type=F32)
             first = n == 0
             own[i, :, at] = jnp.where(first, r[:R2], r[R2:])

time: 52.4 us -> 51.4 us (0.981)
  Pallas kernels: 50.7 us -> 49.7 us
    pallas_call x1, Pallas kernels: 50.7 us -> 49.7 us  [fused(): pl.pallas_call(functools.partial(kernel, W, chunks, down_groups, tiles),...]
where the time goes in v3:
time: 51.4 us; the launch traced here: 51.2 us
  Pallas kernels  49.7 us (97%)
  local copies, waits for them, and re-layouts  1.47 us (3%)
    pallas_call x1, Pallas kernels, fused(): pl.pallas_call(functools.partial(kernel, W, chunks, down_groups, tiles),...  49.7 us
    unnamed x1, local copies, waits for them, and re-layouts  1.47 us

profile of v3, /device:TPU:0, one launch (start us, length us, event | category | flops | bytes accessed | tf_op | source)
XLA Modules:
  0.0 51.2 jit_solution(14649459029910562415)
XLA Ops:
  0.0 49.7 %shard_map.46 = bf16[8,4096]{1,0:T(8,128)(2,1)} custom-call(bf16[8,4096]{1,0:T(8,128)(2,1)} %x_ref.1, bf16[4096,3328]{1,0:T(8,128)(2,1)} %gate_ref.1, bf16[4096,3328]{1,0:T(8,128)(2,1)} %up_ref.1, bf16[3328,4096]{1,0:T(8,128)(2,1)} %down_ref.1), custom_call_target="tpu_custom_call" | custom-call | flops 5234491392 | bytes 40894464 | tf_op jit(solution)/shard_map/pallas_call | solution.py:245
  49.7 1.5 %copy.6 = bf16[8,4096]{1,0:T(8,128)(2,1)} copy(bf16[8,4096]{1,0:T(8,128)(2,1)} %shard_map.46) | data formatting | bytes 131072

commit v4 on v3

--- a/solution.py
+++ b/solution.py
@@ -156,7 +156,7 @@
             if after is not None:
                 after(t)
 
-    lag = 2
+    lag = 3
     C = len(chunks)
     ready = {grp[-1]: i for i, grp in enumerate(down_groups)}
     last = len(down_groups) - 1

time: 51.4 us -> 51.7 us (level)
  no operation moved by 1% of the time
where the time goes in v4:
time: 51.7 us; the launch traced here: 51.5 us
  Pallas kernels  50 us (97%)
  local copies, waits for them, and re-layouts  1.47 us (3%)
    pallas_call x1, Pallas kernels, fused(): pl.pallas_call(functools.partial(kernel, W, chunks, down_groups, tiles),...  50 us
    unnamed x1, local copies, waits for them, and re-layouts  1.47 us

profile of v4, /device:TPU:0, one launch (start us, length us, event | category | flops | bytes accessed | tf_op | source)
XLA Modules:
  0.0 51.5 jit_solution(9809191314287273162)
XLA Ops:
  0.0 50.0 %shard_map.46 = bf16[8,4096]{1,0:T(8,128)(2,1)} custom-call(bf16[8,4096]{1,0:T(8,128)(2,1)} %x_ref.1, bf16[4096,3328]{1,0:T(8,128)(2,1)} %gate_ref.1, bf16[4096,3328]{1,0:T(8,128)(2,1)} %up_ref.1, bf16[3328,4096]{1,0:T(8,128)(2,1)} %down_ref.1), custom_call_target="tpu_custom_call" | custom-call | flops 5234491392 | bytes 40894464 | tf_op jit(solution)/shard_map/pallas_call | solution.py:245
  50.0 1.5 %copy.6 = bf16[8,4096]{1,0:T(8,128)(2,1)} copy(bf16[8,4096]{1,0:T(8,128)(2,1)} %shard_map.46) | data formatting | bytes 131072
